TPU v7x, 768 devices: a whole 4x8x12 slice. The times are simulated.
768 devices in a mesh: sub: 96 (over z, x, core), grp: 8 (over y).
Axes of the slice: x: 4, y: 8, z: 12, core: 2. Of those that a mesh axis runs over, the one named last changes fastest.
Arguments:
- basis: bfloat16 [1536, 64, 4096], P(('sub', 'grp')), may hold values from -3 to 3
- stiffness: bfloat16 [6144, 4, 128, 128], P(('sub', 'grp')), may hold values from -0.5 to 0.5
- pair_subs: int32 [6144, 2], P(('sub', 'grp')), may hold values from 0 to 1
- own_rows: int32 [6144, 4], P(('sub', 'grp')), may hold values from 0 to 31, as said below
- far_rows: int32 [6144, 4], P(('sub', 'grp')), may hold values from 0 to 31, as said below
- pair_count: int32 [768], P(('sub', 'grp')), may hold values from 1 to 8, as said below
Outputs:
- owned_blocks: float32 [6144, 4096], P('sub')
- partner_blocks: float32 [6144, 4096], P('sub')
Inputs may be any that keep to these rules, and one draw needn't show every extreme that they name: `own_rows`: the 4 tiles of one pair are distinct. `far_rows`: the 4 tiles of one pair are distinct. `pair_count`: live slots are the first ones of a device; some device has all 8 live in every draw.
All inputs are finite; a program needn't handle non-finite values.
Results may differ from a plain program's by a relative error of at most 0.0029.
Values may be sent and summed in bfloat16 or wider, within the bound.
No kernel may reach another device: no remote copies, remote signals or barrier semaphores. Data moves between devices by JAX's collectives and lax.ppermute only.
A program may use at most 32 MiB of HBM per device.

v0:
```python
import jax
import jax.numpy as jnp
from jax import lax
from jax.sharding import PartitionSpec as P


def shifted(block, axis, distance):
    devices = range(lax.axis_size(axis))
    route = [((i - distance) % len(devices), i) for i in devices]
    return lax.ppermute(block, axis, route)


def collect(basis_block, sub_choice, margin_tiles):
    basis_width, local_total = (basis_block.shape[1], basis_block.shape[2])
    tiled = basis_block.reshape(basis_block.shape[0], basis_width, local_total // 128, 128)

    def one_pair(s, tiles):
        picked = jnp.take(tiled[s], tiles, axis=1)
        return picked.reshape(basis_width, tiles.shape[0] * 128)

    return jax.vmap(one_pair)(sub_choice, margin_tiles)


def cross_blocks(own_part, far_part, stiff_tiles, live_count):
    pair_total, basis_width, margin_total = far_part.shape
    tile_count = stiff_tiles.shape[1]
    far_tiles = far_part.reshape(pair_total, basis_width, tile_count, margin_total // tile_count)
    stiff_image = jnp.einsum(
        "pntc,ptrc->pntr", far_tiles, stiff_tiles, preferred_element_type=jnp.float32
    ).astype(jnp.bfloat16)
    stiff_image = stiff_image.reshape(pair_total, basis_width, margin_total)
    keep_mask = (jnp.arange(pair_total, dtype=jnp.int32) < live_count).astype(jnp.float32)[
        :, None, None
    ]
    blocks = (
        jnp.einsum("pno,pmo->pnm", own_part, stiff_image, preferred_element_type=jnp.float32)
        * keep_mask
    )
    flipped = (
        jnp.einsum("pmo,pno->pmn", stiff_image, own_part, preferred_element_type=jnp.float32)
        * keep_mask
    )
    return (blocks, flipped)


def on_device(basis, stiffness, pair_subs, own_rows, far_rows, pair_count):
    live_count = pair_count[0]
    own_part = collect(basis, pair_subs[:, 0], own_rows)
    request = jnp.concatenate([far_rows, pair_subs[:, 1:2]], axis=1)
    wanted = shifted(request, "sub", -1)
    served = collect(basis, wanted[:, -1], wanted[:, :-1])
    far_part = shifted(served, "sub", 1)
    blocks, flipped = cross_blocks(own_part, far_part, stiffness, live_count)
    pair_total = blocks.shape[0]
    basis_width = blocks.shape[1]
    flat_blocks = blocks.reshape(pair_total, basis_width * basis_width)
    flat_flipped = flipped.reshape(pair_total, basis_width * basis_width)
    returned = shifted(flat_flipped, "sub", -1)
    owned_all, partner_all = (
        lax.all_gather(flat_blocks, "grp", axis=0, tiled=True),
        lax.all_gather(returned, "grp", axis=0, tiled=True),
    )
    return (owned_all, partner_all)


def solution(mesh):
    return jax.shard_map(
        on_device,
        mesh=mesh,
        in_specs=(
            P(("sub", "grp"), None, None),
            P(("sub", "grp"), None, None, None),
            P(("sub", "grp"), None),
            P(("sub", "grp"), None),
            P(("sub", "grp"), None),
            P(("sub", "grp")),
        ),
        out_specs=(P("sub", None), P("sub", None)),
        check_vma=False,
    )
```

profile of v0, /device:TPU:6, one launch (start us, length us, event | category | flops | bytes accessed | tf_op | source)
XLA Modules:
  0.0 143.8 jit_solution(9020711612019602)
XLA Ops:
  7.2 0.8 fusion.14
  8.0 0.7 pad_add_fusion
  8.7 2.2 %collective-permute-start = (s32[8,5]{0,1:T(8,128)S(1)}, s32[8,5]{0,1:T(8,128)S(1)}, u32[]{:S(2)}, u32[]{:S(2)}) collective-permute-start(s32[8,5]{0,1:T(8,128)S(1)} %pad_add_fusion), channel_id=1, source_target_pairs={{8,0},{16,8},{24,16},{32,24},{40,32},{48,40},{56,48},{64,56},{72,6... | collective-permute-start | bytes 488 | tf_op jit(solution)/shard_map/ppermute | solution.py:10
  10.9 0.3 copy_bitcast_fusion
  11.8 0.4 collective-permute-done
  12.5 3.0 %gather_fusion.1 = bf16[8,64,32,128]{3,1,2,0:T(8,128)(2,1)} fusion(bf16[2,64,32,128]{3,1,2,0:T(8,128)(2,1)S(1)} %copy_bitcast_fusion, s32[8]{0:T(128)S(1)} %fusion.17), kind=kCustom, calls=%fused_computation.3 | custom fusion | bytes 8388736 | tf_op jit(solution)/shard_map/vmap()/gather | solution.py:18
  15.5 2.9 %gather_fusion.3 = bf16[32,64,128]{2,1,0:T(8,128)(2,1)S(1)} fusion(bf16[8,64,32,128]{3,1,2,0:T(8,128)(2,1)} %gather_fusion.1, s32[32]{0:T(128)S(1)} %reshape.87), kind=kCustom, calls=%fused_computation.1.clone | custom fusion | bytes 1048832 | tf_op jit(solution)/shard_map/vmap(jit(_take))/gather | solution.py:18
  18.4 0.5 fusion.7
  18.8 1.0 reshape.38
  19.8 5.3 %collective-permute-start.1 = (bf16[8,64,512]{2,1,0:T(8,128)(2,1)}, bf16[8,64,512]{2,1,0:T(8,128)(2,1)}, u32[]{:S(2)}, u32[]{:S(2)}) collective-permute-start(bf16[8,64,512]{2,1,0:T(8,128)(2,1)} %reshape.38), channel_id=1, source_target_pairs={{760,0},{0,8},{8,16},{16,24},{24,32},{32,40},{40,48},{48,56},{56,6... | collective-permute-start | bytes 1572872 | tf_op jit(solution)/shard_map/ppermute | solution.py:10
  25.4 3.0 %gather_fusion = bf16[8,64,32,128]{3,1,2,0:T(8,128)(2,1)} fusion(bf16[2,64,32,128]{3,1,2,0:T(8,128)(2,1)S(1)} %copy_bitcast_fusion, s32[8]{0:T(128)S(1)} %get-tuple-element.3), kind=kCustom, calls=%fused_computation.2 | custom fusion | bytes 8388736 | tf_op jit(solution)/shard_map/vmap()/gather | solution.py:18
  28.5 2.9 %gather_fusion.2 = bf16[32,64,128]{2,1,0:T(8,128)(2,1)S(1)} fusion(bf16[8,64,32,128]{3,1,2,0:T(8,128)(2,1)} %gather_fusion, s32[32]{0:T(128)S(1)} %reshape.82), kind=kCustom, calls=%fused_computation.clone | custom fusion | bytes 1048832 | tf_op jit(solution)/shard_map/vmap(jit(_take))/gather | solution.py:18
  31.3 1.9 %fusion = bf16[8,4,8,8,128]{4,3,2,1,0:T(8,128)(2,1)S(1)} fusion(bf16[8,4,128,128]{3,2,1,0:T(8,128)(2,1)S(1)} %copy-done.1, bf16[8,64,512]{2,1,0:T(8,128)(2,1)} %collective-permute-done.1), kind=kOutput, calls=%fused_computation.5 | convolution fusion | flops 67371008 | bytes 2097152 | tf_op jit(solution)/shard_map/pntc,ptrc->pntr/dot_general | solution.py:28
  33.2 0.4 convolution_multiply_fusion.1
  33.6 0.8 reshape.41
  34.4 0.4 convolution_multiply_fusion
  34.8 0.1 reshape.42
  34.9 1.9 %collective-permute-start.2 = (f32[8,4096]{1,0:T(8,128)S(1)}, f32[8,4096]{1,0:T(8,128)S(1)}, u32[]{:S(2)}, u32[]{:S(2)}) collective-permute-start(f32[8,4096]{1,0:T(8,128)S(1)} %reshape.42), channel_id=1, source_target_pairs={{8,0},{16,8},{24,16},{32,24},{40,32},{48,40},{56,48},{64,56},{72,6... | collective-permute-start | bytes 393224 | tf_op jit(solution)/shard_map/ppermute | solution.py:10
  36.8 2.5 %collective-permute-done.2 = f32[8,4096]{1,0:T(8,128)S(1)} collective-permute-done((f32[8,4096]{1,0:T(8,128)S(1)}, f32[8,4096]{1,0:T(8,128)S(1)}, u32[]{:S(2)}, u32[]{:S(2)}) %collective-permute-start.2) | collective-permute-done | bytes 131104 | tf_op jit(solution)/shard_map/ppermute | solution.py:10
  39.3 0.7 copy-done.2
  40.0 46.9 %all-gather.3.cloned.1.call-done = f32[64,4096]{1,0:T(8,128)} async-done(((f32[8,4096]{1,0:T(8,128)}), f32[64,4096]{1,0:T(8,128)}) %all-gather.3.cloned.1.call-update) | async-done | bytes 1048592 | tf_op jit(solution)/shard_map/all_gather | solution.py:60
  86.9 45.5 %all-gather.5.cloned.1.call-done = f32[64,4096]{1,0:T(8,128)} async-done(((f32[8,4096]{1,0:T(8,128)}), f32[64,4096]{1,0:T(8,128)}) %all-gather.5.cloned.1.call-update) | async-done | bytes 1048592 | tf_op jit(solution)/shard_map/all_gather | solution.py:61
  132.4 2.3 %copy.54 = f32[64,4096]{1,0:T(8,128)} copy(f32[64,4096]{1,0:T(8,128)} %all-gather.3.cloned.1.call-done) | data formatting | bytes 2097152
  134.7 2.3 %copy.55 = f32[64,4096]{1,0:T(8,128)} copy(f32[64,4096]{1,0:T(8,128)} %all-gather.5.cloned.1.call-done) | data formatting | bytes 2097152
  (24 shorter events, 0.7 us)
Async XLA Ops:
  7.2 3.7 %copy-start = (bf16[2,64,4096]{2,1,0:T(8,128)(2,1)S(1)}, bf16[2,64,4096]{2,1,0:T(8,128)(2,1)}, u32[]{:S(2)}) copy-start(bf16[2,64,4096]{2,1,0:T(8,128)(2,1)} %param.8) | copy-start | bytes 3145732
  7.2 79.7 %all-gather.3.cloned.1.call-start = ((), (), s32[]{:S(2)}) async-start(), calls=%async_computation | async-start | bytes 1179648 | tf_op jit(solution)/shard_map/all_gather | solution.py:60
  8.7 3.5 %collective-permute-start = (s32[8,5]{0,1:T(8,128)S(1)}, s32[8,5]{0,1:T(8,128)S(1)}, u32[]{:S(2)}, u32[]{:S(2)}) collective-permute-start(s32[8,5]{0,1:T(8,128)S(1)} %pad_add_fusion), channel_id=1, source_target_pairs={{8,0},{16,8},{24,16},{32,24},{40,32},{48,40},{56,48},{64,56},{72,6... | collective-permute-start | bytes 488 | tf_op jit(solution)/shard_map/ppermute | solution.py:10
  12.5 12.7 %copy-start.3 = (s32[8,4]{0,1:T(4,128)S(1)}, s32[8,4]{0,1:T(4,128)}, u32[]{:S(2)}) copy-start(s32[8,4]{0,1:T(4,128)} %param.11) | copy-start | bytes 388
  19.8 11.5 %collective-permute-start.1 = (bf16[8,64,512]{2,1,0:T(8,128)(2,1)}, bf16[8,64,512]{2,1,0:T(8,128)(2,1)}, u32[]{:S(2)}, u32[]{:S(2)}) collective-permute-start(bf16[8,64,512]{2,1,0:T(8,128)(2,1)} %reshape.38), channel_id=1, source_target_pairs={{760,0},{0,8},{8,16},{16,24},{24,32},{32,40},{40,48},{48,56},{56,6... | collective-permute-start | bytes 1572872 | tf_op jit(solution)/shard_map/ppermute | solution.py:10
  25.4 5.9 %copy-start.1 = (bf16[8,4,128,128]{3,2,1,0:T(8,128)(2,1)S(1)}, bf16[8,4,128,128]{3,2,1,0:T(8,128)(2,1)}, u32[]{:S(2)}) copy-start(bf16[8,4,128,128]{3,2,1,0:T(8,128)(2,1)} %param.9) | copy-start | bytes 3145732
  34.4 98.1 %all-gather.5.cloned.1.call-start = ((), (), s32[]{:S(2)}) async-start(), calls=%async_computation.1 | async-start | bytes 1179648 | tf_op jit(solution)/shard_map/all_gather | solution.py:61
  34.9 4.4 %collective-permute-start.2 = (f32[8,4096]{1,0:T(8,128)S(1)}, f32[8,4096]{1,0:T(8,128)S(1)}, u32[]{:S(2)}, u32[]{:S(2)}) collective-permute-start(f32[8,4096]{1,0:T(8,128)S(1)} %reshape.42), channel_id=1, source_target_pairs={{8,0},{16,8},{24,16},{32,24},{40,32},{48,40},{56,48},{64,56},{72,6... | collective-permute-start | bytes 393224 | tf_op jit(solution)/shard_map/ppermute | solution.py:10
  39.3 0.7 copy-start.2
Sparse Core Ops, SparseCore 0:
  34.5 52.3 all-gather.2
  89.8 42.5 all-gather.4
where the time goes:
time: 144 us
  waiting for transfers between devices  95.3 us (66%)
  local copies, waits for them, and re-layouts  19.7 us (14%)
  between operations  14.8 us (10%)
  starting transfers between devices  9.44 us (7%)
  matrix products  2.58 us (2%)
  other arithmetic  1.97 us (1%)
    all_gather x1, waiting for transfers between devices, on_device(): lax.all_gather(flat_blocks, 'grp', axis=0, tiled=True)  46.9 us
    all_gather x1, waiting for transfers between devices, on_device(): lax.all_gather(returned, 'grp', axis=0, tiled=True)  45.5 us
    gather x8, local copies, waits for them, and re-layouts, one_pair(): picked = jnp.take(tiled[s], tiles, axis=1)  12.1 us
    ppermute x3, starting transfers between devices, shifted(): return lax.ppermute(block, axis, route)  9.36 us
    unnamed x10, local copies, waits for them, and re-layouts  5.21 us
  transfers between devices with their start and end apart: 5, of which 4 were waited for; matrix products, arithmetic and copies ran while one was open for 5% of the time, Pallas kernels for 0%

commit v1 on v0

v1 whole, which is shorter than its diff:
```python
import jax
import jax.numpy as jnp
from jax import lax
from jax.experimental import pallas as pl
from jax.experimental.pallas import tpu as pltpu
from jax.sharding import PartitionSpec as P

VMEM_LIMIT = 16 * 1024 * 1024


def shifted(block, axis, distance):
    devices = range(lax.axis_size(axis))
    route = [((i - distance) % len(devices), i) for i in devices]
    return lax.ppermute(block, axis, route)


def collect_kernel(wanted_ref, basis_ref, part_ref, sems):
    pair_total, tile_count = wanted_ref.shape
    tile_total = basis_ref.shape[2] // 128
    copies = []
    for p in range(pair_total):
        for t in range(tile_count):
            code = wanted_ref[p, t]
            s = code // tile_total
            first = pl.multiple_of((code - s * tile_total) * 128, 128)
            copy = pltpu.make_async_copy(
                basis_ref.at[s, :, pl.ds(first, 128)],
                part_ref.at[p, :, pl.ds(t * 128, 128)],
                sems.at[p, t],
            )
            copy.start()
            copies.append(copy)
    for copy in copies:
        copy.wait()


def collect(basis, wanted):
    pair_total, tile_count = wanted.shape
    shape = (pair_total, basis.shape[1], tile_count * 128)
    return pl.pallas_call(
        collect_kernel,
        out_shape=jax.ShapeDtypeStruct(shape, basis.dtype),
        in_specs=[
            pl.BlockSpec(memory_space=pltpu.SMEM),
            pl.BlockSpec(memory_space=pl.ANY),
        ],
        out_specs=pl.BlockSpec(memory_space=pl.ANY),
        scratch_shapes=[pltpu.SemaphoreType.DMA((pair_total, tile_count))],
        compiler_params=pltpu.CompilerParams(vmem_limit_bytes=VMEM_LIMIT),
        cost_estimate=pl.CostEstimate(flops=0, bytes_accessed=2**20, transcendentals=0),
        name="collect",
    )(wanted, basis)


def flat_rows(rows_ref, width):
    left = lax.broadcasted_iota(jnp.int32, (8, 2 * width), 1) < width
    for k in range(width // 2):
        even = rows_ref[pl.ds(2 * k, 8, stride=width), :]
        odd = rows_ref[pl.ds(2 * k + 1, 8, stride=width), :]
        yield k, jnp.where(left, even, odd)


NT = (((1,), (1,)), ((), ()))


def cross_kernel(count_ref, own_ref, far_ref, stiff_ref, out_ref, rows_ref):
    pair_total, width, _ = far_ref.shape
    tile_count = stiff_ref.shape[1]
    live = count_ref[0]
    for p in range(pair_total):
        image = jnp.concatenate(
            [
                lax.dot_general(
                    far_ref[p, :, t * 128 : (t + 1) * 128],
                    stiff_ref[p, t],
                    NT,
                    preferred_element_type=jnp.float32,
                ).astype(jnp.bfloat16)
                for t in range(tile_count)
            ],
            axis=1,
        )
        own = own_ref[p]
        flipped = lax.dot_general(
            image,
            jnp.concatenate([own, own], axis=0),
            NT,
            preferred_element_type=jnp.float32,
        )
        rows_ref[p * width : (p + 1) * width, :] = jnp.where(p < live, flipped, 0.0)
    for k, row in flat_rows(rows_ref, width):
        row = row.astype(out_ref.dtype)
        for d in range(out_ref.shape[0]):
            out_ref[d, :, 2 * width * k : 2 * width * (k + 1)] = row


def cross_blocks(live, own_part, far_part, stiffness, copies):
    pair_total, width, _ = far_part.shape
    vmem = pl.BlockSpec(memory_space=pltpu.VMEM)
    return pl.pallas_call(
        cross_kernel,
        out_shape=jax.ShapeDtypeStruct((copies, pair_total, width * width), jnp.bfloat16),
        in_specs=[pl.BlockSpec(memory_space=pltpu.SMEM), vmem, vmem, vmem],
        out_specs=vmem,
        scratch_shapes=[pltpu.VMEM((pair_total * width, 2 * width), jnp.float32)],
        compiler_params=pltpu.CompilerParams(vmem_limit_bytes=VMEM_LIMIT),
        cost_estimate=pl.CostEstimate(flops=2**27, bytes_accessed=2**21, transcendentals=0),
        name="cross_blocks",
    )(live, own_part, far_part, stiffness)


def turn_kernel(flat_ref, out_ref, split_ref, rows_ref):
    group_total, pair_total, flat_width = flat_ref.shape
    width = rows_ref.shape[1] // 2
    row_at = lax.broadcasted_iota(jnp.int32, (width, 2 * width), 0)
    lane_at = lax.broadcasted_iota(jnp.int32, (width, 2 * width), 1)
    pick = (row_at == lane_at).astype(jnp.bfloat16)

    @pl.loop(0, group_total)
    def _(g):
        for k in range(width // 2):
            both = flat_ref[g, :, 2 * width * k : 2 * width * (k + 1)].astype(jnp.float32)
            split_ref[pl.ds(2 * k, 8, stride=width), :] = both
            split_ref[pl.ds(2 * k + 1, 8, stride=width), :] = pltpu.roll(both, width, 1)
        for p in range(pair_total):
            matrix = split_ref[p * width : (p + 1) * width, :].astype(jnp.bfloat16)
            rows_ref[p * width : (p + 1) * width, :] = lax.dot_general(
                pick,
                jnp.concatenate([matrix, matrix], axis=0),
                NT,
                preferred_element_type=jnp.float32,
            )
        first = pl.multiple_of(g * pair_total, pair_total)
        for k, row in flat_rows(rows_ref, width):
            out_ref[pl.ds(first, pair_total), 2 * width * k : 2 * width * (k + 1)] = row


def turned(flat, width):
    group_total, pair_total, flat_width = flat.shape
    vmem = pl.BlockSpec(memory_space=pltpu.VMEM)
    scratch = pltpu.VMEM((pair_total * width, 2 * width), jnp.float32)
    return pl.pallas_call(
        turn_kernel,
        out_shape=jax.ShapeDtypeStruct((group_total * pair_total, flat_width), jnp.float32),
        in_specs=[vmem],
        out_specs=vmem,
        scratch_shapes=[scratch, scratch],
        compiler_params=pltpu.CompilerParams(vmem_limit_bytes=VMEM_LIMIT),
        cost_estimate=pl.CostEstimate(flops=2**27, bytes_accessed=2**21, transcendentals=0),
        name="turned",
    )(flat)


def on_device(basis, stiffness, pair_subs, own_rows, far_rows, pair_count):
    tile_total = basis.shape[2] // 128
    width = basis.shape[1]
    wanted = shifted(far_rows + pair_subs[:, 1:2] * tile_total, "sub", -1)
    own_part = collect(basis, own_rows + pair_subs[:, 0:1] * tile_total)
    far_part = shifted(collect(basis, wanted), "sub", 1)
    groups = lax.axis_size("grp")
    flipped = cross_blocks(pair_count, own_part, far_part, stiffness, groups)
    gathered = lax.all_to_all(flipped, "grp", 0, 0)
    returned = shifted(gathered, "sub", -1)
    owned_all = turned(gathered, width)
    partner_all = returned.reshape(owned_all.shape).astype(jnp.float32)
    return (owned_all, partner_all)


def solution(mesh):
    return jax.shard_map(
        on_device,
        mesh=mesh,
        in_specs=(
            P(("sub", "grp"), None, None),
            P(("sub", "grp"), None, None, None),
            P(("sub", "grp"), None),
            P(("sub", "grp"), None),
            P(("sub", "grp"), None),
            P(("sub", "grp")),
        ),
        out_specs=(P("sub", None), P("sub", None)),
        check_vma=False,
    )
```

time: 144 us -> 69 us (0.48)
  the two profiles are of different devices: /device:TPU:6 before, /device:TPU:8 now
where the time goes in v1:
time: 69 us; the launch traced here: 68.7 us
  starting transfers between devices  22.7 us (33%)
  blocking collectives  19.2 us (28%)
  waiting for transfers between devices  12.4 us (18%)
  Pallas kernels  9.7 us (14%)
  other arithmetic  1.94 us (3%)
  local copies, waits for them, and re-layouts  1.4 us (2%)
  between operations  1.36 us (2%)
    ppermute x3, starting transfers between devices, shifted(): return lax.ppermute(block, axis, route)  22.7 us
    all_to_all x1, blocking collectives, on_device(): gathered = lax.all_to_all(flipped, 'grp', 0, 0)  19.2 us
    ppermute x3, waiting for transfers between devices, shifted(): return lax.ppermute(block, axis, route)  12.4 us
    pallas_call x1, Pallas kernels, turned(): pl.pallas_call(turn_kernel, out_shape=jax.ShapeDtypeStruct((group_total *...  5.2 us
    pallas_call x2, Pallas kernels, collect(): pl.pallas_call(collect_kernel, out_shape=jax.ShapeDtypeStruct(shape, basi...  2.98 us
    pallas_call x1, Pallas kernels, cross_blocks(): pl.pallas_call(cross_kernel, out_shape=jax.ShapeDtypeStruct((copies, pair...  1.52 us
    unnamed x12, local copies, waits for them, and re-layouts  1.4 us
  transfers between devices with their start and end apart: 3, of which 3 were waited for; matrix products, arithmetic and copies ran while one was open for 0% of the time, Pallas kernels for 10%

profile of v1, /device:TPU:8, one launch (start us, length us, event | category | flops | bytes accessed | tf_op | source)
XLA Modules:
  0.0 68.7 jit_solution(5126598687729002164)
XLA Ops:
  0.6 0.0 copy-start.3
  0.6 0.8 %multiply_bitcast_fusion = (s32[8]{0:T(128)S(1)}, s32[8]{0:T(128)S(1)}) fusion(s32[8,2]{0,1:T(2,128)} %param.8), kind=kLoop, calls=%fused_computation.3 | loop fusion | flops 16 | bytes 128 | tf_op jit(solution)/shard_map/add | solution.py:157
  1.4 0.0 copy-done.3
  1.4 0.1 copy.9
  1.5 0.1 broadcast_add_fusion
  1.6 16.2 %collective-permute-start = (s32[8,4]{1,0:T(8,128)S(1)}, s32[8,4]{1,0:T(8,128)S(1)}, u32[]{:S(2)}, u32[]{:S(2)}) collective-permute-start(s32[8,4]{1,0:T(8,128)S(1)} %broadcast_add_fusion), channel_id=1, source_target_pairs={{8,0},{16,8},{24,16},{32,24},{40,32},{48,40},{56,48},{64,56},{72,6... | collective-permute-start | bytes 392 | tf_op jit(solution)/shard_map/ppermute | solution.py:14
  17.8 1.3 %collective-permute-done.wanted_ref = s32[8,4]{1,0:T(8,128)S(1)} collective-permute-done((s32[8,4]{1,0:T(8,128)S(1)}, s32[8,4]{1,0:T(8,128)S(1)}, u32[]{:S(2)}, u32[]{:S(2)}) %collective-permute-start) | collective-permute-done | bytes 160 | tf_op jit(solution)/shard_map/ppermute | solution.py:14
  19.1 1.2 %copy-done = bf16[2,64,4096]{2,1,0:T(8,128)(2,1)S(1)} copy-done((bf16[2,64,4096]{2,1,0:T(8,128)(2,1)S(1)}, bf16[2,64,4096]{2,1,0:T(8,128)(2,1)}, u32[]{:S(2)}) %copy-start) | copy-done | bytes 1048600
  20.3 1.5 %collect.3 = bf16[8,64,512]{2,1,0:T(8,128)(2,1)S(1)} custom-call(s32[8,4]{1,0:T(8,128)S(1)} %collective-permute-done.wanted_ref, bf16[2,64,4096]{2,1,0:T(8,128)(2,1)S(1)} %copy-done), custom_call_target="tpu_custom_call" | custom-call | bytes 1048576 | tf_op jit(solution)/shard_map/collect/pallas_call | solution.py:40
  21.8 0.0 copy-start.2
  21.8 2.1 %collective-permute-start.1 = (bf16[8,64,512]{2,1,0:T(8,128)(2,1)S(1)}, bf16[8,64,512]{2,1,0:T(8,128)(2,1)S(1)}, u32[]{:S(2)}, u32[]{:S(2)}) collective-permute-start(bf16[8,64,512]{2,1,0:T(8,128)(2,1)S(1)} %collect.3), channel_id=1, source_target_pairs={{760,0},{0,8},{8,16},{16,24},{24,32},{32,40},{40,48},{48,56},{56,6... | collective-permute-start | bytes 1572872 | tf_op jit(solution)/shard_map/ppermute | solution.py:14
  24.5 0.0 copy-done.4
  24.5 0.1 copy.8
  24.6 0.1 broadcast_add_fusion.1.wanted_ref
  24.7 0.0 copy-done.1
  24.7 1.5 %collect.2.own_ref = bf16[8,64,512]{2,1,0:T(8,128)(2,1)S(1)} custom-call(s32[8,4]{1,0:T(8,128)S(1)} %broadcast_add_fusion.1.wanted_ref, bf16[2,64,4096]{2,1,0:T(8,128)(2,1)S(1)} %copy-done.1), custom_call_target="tpu_custom_call" | custom-call | bytes 1048576 | tf_op jit(solution)/shard_map/collect/pallas_call | solution.py:40
  26.2 9.6 %collective-permute-done.1.far_ref = bf16[8,64,512]{2,1,0:T(8,128)(2,1)S(1)} collective-permute-done((bf16[8,64,512]{2,1,0:T(8,128)(2,1)S(1)}, bf16[8,64,512]{2,1,0:T(8,128)(2,1)S(1)}, u32[]{:S(2)}, u32[]{:S(2)}) %collective-permute-start.1) | collective-permute-done | bytes 524320 | tf_op jit(solution)/shard_map/ppermute | solution.py:14
  35.8 0.0 copy-done.2
  35.8 1.5 %cross_blocks.1 = bf16[8,8,4096]{2,1,0:T(8,128)(2,1)S(1)} custom-call(s32[1]{0:T(128)S(6)} %copy.10.count_ref, bf16[8,64,512]{2,1,0:T(8,128)(2,1)S(1)} %collect.2.own_ref, bf16[8,64,512]{2,1,0:T(8,128)(2,1)S(1)} %collective-permute-done.1.far_ref, bf16[8,4,128,128]{3,2,1,0:T(8,128)(2,1)S(1)} %copy-done.2), custom_call_target="tpu_custom_call" | custom-call | flops 134217728 | bytes 2097152 | tf_op jit(solution)/shard_map/cross_blocks/pallas_call | solution.py:100
  37.3 19.2 %all_to_all.5.flat_ref = bf16[8,8,4096]{2,1,0:T(8,128)(2,1)S(1)} all-to-all(bf16[8,8,4096]{2,1,0:T(8,128)(2,1)S(1)} %cross_blocks.1), channel_id=1, replica_groups=mesh['sub'=96,'grp'=8] {'grp'}, dimensions={0} | all-to-all | bytes 1048576 | tf_op jit(solution)/shard_map/all_to_all | solution.py:162
  56.5 4.4 %collective-permute-start.2 = (bf16[8,8,4096]{2,1,0:T(8,128)(2,1)S(1)}, bf16[8,8,4096]{2,1,0:T(8,128)(2,1)S(1)}, u32[]{:S(2)}, u32[]{:S(2)}) collective-permute-start(bf16[8,8,4096]{2,1,0:T(8,128)(2,1)S(1)} %all_to_all.5.flat_ref), channel_id=1, source_target_pairs={{8,0},{16,8},{24,16},{32,24},{40,32},{48,40},{56,48},{64,56},{72,6... | collective-permute-start | bytes 1572872 | tf_op jit(solution)/shard_map/ppermute | solution.py:14
  60.9 5.2 %turned.1 = f32[64,4096]{1,0:T(8,128)} custom-call(bf16[8,8,4096]{2,1,0:T(8,128)(2,1)S(1)} %all_to_all.5.flat_ref), custom_call_target="tpu_custom_call" | custom-call | flops 134217728 | bytes 2097152 | tf_op jit(solution)/shard_map/turned/pallas_call | solution.py:142
  66.1 1.5 %collective-permute-done.2 = bf16[8,8,4096]{2,1,0:T(8,128)(2,1)S(1)} collective-permute-done((bf16[8,8,4096]{2,1,0:T(8,128)(2,1)S(1)}, bf16[8,8,4096]{2,1,0:T(8,128)(2,1)S(1)}, u32[]{:S(2)}, u32[]{:S(2)}) %collective-permute-start.2) | collective-permute-done | bytes 524320 | tf_op jit(solution)/shard_map/ppermute | solution.py:14
  67.6 1.0 %bitcast_convert_fusion = f32[64,4096]{1,0:T(8,128)} fusion(bf16[8,8,4096]{2,1,0:T(8,128)(2,1)S(1)} %collective-permute-done.2), kind=kLoop, calls=%fused_computation | loop fusion | flops 262144 | bytes 1572864 | tf_op jit(solution)/shard_map/convert_element_type | solution.py:165
  (3 shorter events, 0.0 us)
Async XLA Ops:
  0.6 0.8 %copy-start.3 = (s32[8,4]{0,1:T(4,128)S(1)}, s32[8,4]{0,1:T(4,128)}, u32[]{:S(2)}) copy-start(s32[8,4]{0,1:T(4,128)} %param.10) | copy-start | bytes 388
  1.6 17.5 %collective-permute-start = (s32[8,4]{1,0:T(8,128)S(1)}, s32[8,4]{1,0:T(8,128)S(1)}, u32[]{:S(2)}, u32[]{:S(2)}) collective-permute-start(s32[8,4]{1,0:T(8,128)S(1)} %broadcast_add_fusion), channel_id=1, source_target_pairs={{8,0},{16,8},{24,16},{32,24},{40,32},{48,40},{56,48},{64,56},{72,6... | collective-permute-start | bytes 392 | tf_op jit(solution)/shard_map/ppermute | solution.py:14
  19.1 1.2 %copy-start = (bf16[2,64,4096]{2,1,0:T(8,128)(2,1)S(1)}, bf16[2,64,4096]{2,1,0:T(8,128)(2,1)}, u32[]{:S(2)}) copy-start(bf16[2,64,4096]{2,1,0:T(8,128)(2,1)} %basis_ref.3) | copy-start | bytes 3145732
  20.3 4.2 %copy-start.4 = (s32[8,4]{0,1:T(4,128)S(1)}, s32[8,4]{0,1:T(4,128)}, u32[]{:S(2)}) copy-start(s32[8,4]{0,1:T(4,128)} %param.9) | copy-start | bytes 388
  20.3 4.4 %copy-start.1 = (bf16[2,64,4096]{2,1,0:T(8,128)(2,1)S(1)}, bf16[2,64,4096]{2,1,0:T(8,128)(2,1)}, u32[]{:S(2)}) copy-start(bf16[2,64,4096]{2,1,0:T(8,128)(2,1)} %basis_ref.3) | copy-start | bytes 3145732
  21.8 14.0 %copy-start.2 = (bf16[8,4,128,128]{3,2,1,0:T(8,128)(2,1)S(1)}, bf16[8,4,128,128]{3,2,1,0:T(8,128)(2,1)}, u32[]{:S(2)}) copy-start(bf16[8,4,128,128]{3,2,1,0:T(8,128)(2,1)} %stiff_ref.1) | copy-start | bytes 3145732
  21.8 14.0 %collective-permute-start.1 = (bf16[8,64,512]{2,1,0:T(8,128)(2,1)S(1)}, bf16[8,64,512]{2,1,0:T(8,128)(2,1)S(1)}, u32[]{:S(2)}, u32[]{:S(2)}) collective-permute-start(bf16[8,64,512]{2,1,0:T(8,128)(2,1)S(1)} %collect.3), channel_id=1, source_target_pairs={{760,0},{0,8},{8,16},{16,24},{24,32},{32,40},{40,48},{48,56},{56,6... | collective-permute-start | bytes 1572872 | tf_op jit(solution)/shard_map/ppermute | solution.py:14
  56.5 11.1 %collective-permute-start.2 = (bf16[8,8,4096]{2,1,0:T(8,128)(2,1)S(1)}, bf16[8,8,4096]{2,1,0:T(8,128)(2,1)S(1)}, u32[]{:S(2)}, u32[]{:S(2)}) collective-permute-start(bf16[8,8,4096]{2,1,0:T(8,128)(2,1)S(1)} %all_to_all.5.flat_ref), channel_id=1, source_target_pairs={{8,0},{16,8},{24,16},{32,24},{40,32},{48,40},{56,48},{64,56},{72,6... | collective-permute-start | bytes 1572872 | tf_op jit(solution)/shard_map/ppermute | solution.py:14

commit v2 on v1

v2 whole, which is shorter than its diff:
```python
import jax
import jax.numpy as jnp
from jax import lax
from jax.experimental import pallas as pl
from jax.experimental.pallas import tpu as pltpu
from jax.sharding import PartitionSpec as P

VMEM_LIMIT = 16 * 1024 * 1024


def shifted(block, axis, distance):
    devices = range(lax.axis_size(axis))
    route = [((i - distance) % len(devices), i) for i in devices]
    return lax.ppermute(block, axis, route)


NT = (((1,), (1,)), ((), ()))
PITCH = 72


def flat_rows(rows_ref, width):
    left = lax.broadcasted_iota(jnp.int32, (8, 2 * width), 1) < width
    for k in range(width // 2):
        even = rows_ref[pl.ds(2 * k, 8, stride=PITCH), :]
        odd = rows_ref[pl.ds(2 * k + 1, 8, stride=PITCH), :]
        yield k, jnp.where(left, even, odd)


OWN_SUB, FAR_SUB, OWN_TILES, FAR_TILES, LIVE = 0, 1, 2, 6, 10


def planned(pair_subs, own_rows, far_rows, pair_count):
    pair_total = own_rows.shape[0]
    live = jnp.broadcast_to(pair_count[:, None], (1, pair_total))
    return jnp.concatenate([pair_subs.T, own_rows.T, far_rows.T, live], axis=0)


def tile(basis_ref, plan_ref, sub_at, tile_at, p):
    first = pl.multiple_of(plan_ref[tile_at, p] * 128, 128)
    return basis_ref[plan_ref[sub_at, p], :, pl.ds(first, 128)]


def collect_kernel(plan_ref, basis_ref, part_ref):
    pair_total, _, margin = part_ref.shape
    for p in range(pair_total):
        for t in range(margin // 128):
            part_ref[p, :, t * 128 : (t + 1) * 128] = tile(
                basis_ref, plan_ref, OWN_SUB, OWN_TILES + t, p
            )


def collect(plan, basis, tile_count):
    vmem = pl.BlockSpec(memory_space=pltpu.VMEM)
    shape = (plan.shape[1], basis.shape[1], tile_count * 128)
    return pl.pallas_call(
        collect_kernel,
        out_shape=jax.ShapeDtypeStruct(shape, basis.dtype),
        in_specs=[pl.BlockSpec(memory_space=pltpu.SMEM), vmem],
        out_specs=vmem,
        compiler_params=pltpu.CompilerParams(vmem_limit_bytes=VMEM_LIMIT),
        cost_estimate=pl.CostEstimate(flops=2**27, bytes_accessed=2**22, transcendentals=0),
        name="collect",
    )(plan, basis)


def cross_kernel(plan_ref, own_ref, far_ref, stiff_ref, out_ref, rows_ref):
    pair_total, tile_count = stiff_ref.shape[:2]
    width = far_ref.shape[1]

    def imaged(p):
        return jnp.concatenate(
            [
                lax.dot_general(
                    tile(far_ref, plan_ref, FAR_SUB, FAR_TILES + t, p),
                    stiff_ref[p, t],
                    NT,
                    preferred_element_type=jnp.float32,
                ).astype(jnp.bfloat16)
                for t in range(tile_count)
            ],
            axis=1,
        )

    def crossed(p, image):
        own = own_ref[p]
        flipped = lax.dot_general(
            image,
            jnp.concatenate([own, own], axis=0),
            NT,
            preferred_element_type=jnp.float32,
        )
        keep = p < plan_ref[LIVE, p]
        rows_ref[p * PITCH : p * PITCH + width, :] = jnp.where(keep, flipped, 0.0)

    image = imaged(0)
    for p in range(pair_total):
        later = imaged(p + 1) if p + 1 < pair_total else None
        crossed(p, image)
        image = later
    for k, row in flat_rows(rows_ref, width):
        row = row.astype(out_ref.dtype)
        for d in range(out_ref.shape[0]):
            out_ref[d, :, 2 * width * k : 2 * width * (k + 1)] = row


def cross_blocks(plan, own_part, far_basis, stiffness, copies):
    pair_total, width, _ = own_part.shape
    vmem = pl.BlockSpec(memory_space=pltpu.VMEM)
    return pl.pallas_call(
        cross_kernel,
        out_shape=jax.ShapeDtypeStruct((copies, pair_total, width * width), jnp.bfloat16),
        in_specs=[pl.BlockSpec(memory_space=pltpu.SMEM), vmem, vmem, vmem],
        out_specs=vmem,
        scratch_shapes=[pltpu.VMEM((pair_total * PITCH, 2 * width), jnp.float32)],
        compiler_params=pltpu.CompilerParams(vmem_limit_bytes=VMEM_LIMIT),
        cost_estimate=pl.CostEstimate(flops=2**27, bytes_accessed=2**21, transcendentals=0),
        name="cross_blocks",
    )(plan, own_part, far_basis, stiffness)


ORDER = [5, 4, 6, 3, 7, 2, 0, 1]


def rows_copy(held_ref, out_ref, sems, g):
    pair_total = held_ref.shape[1]
    first = ORDER[g] * pair_total
    return pltpu.make_async_copy(
        held_ref.at[g], out_ref.at[pl.ds(first, pair_total), :], sems.at[g]
    )


LANES = 4


def turn_kernel(flat_ref, out_ref, held_ref, sems, *scratch):
    group_total, pair_total, _ = flat_ref.shape
    width = scratch[0].shape[1] // 2
    row_at = lax.broadcasted_iota(jnp.int32, (width, 2 * width), 0)
    lane_at = lax.broadcasted_iota(jnp.int32, (width, 2 * width), 1)
    pick = (row_at == lane_at).astype(jnp.bfloat16)

    for g in range(group_total):
        split_ref, rows_ref = scratch[2 * (g % LANES) : 2 * (g % LANES) + 2]
        for k in range(width // 2):
            both = flat_ref[g, :, 2 * width * k : 2 * width * (k + 1)].astype(jnp.float32)
            split_ref[pl.ds(2 * k, 8, stride=PITCH), :] = both
            split_ref[pl.ds(2 * k + 1, 8, stride=PITCH), :] = pltpu.roll(both, width, 1)
        for p in range(pair_total):
            here = slice(p * PITCH, p * PITCH + width)
            matrix = split_ref[here, :].astype(jnp.bfloat16)
            rows_ref[here, :] = lax.dot_general(
                pick,
                jnp.concatenate([matrix, matrix], axis=0),
                NT,
                preferred_element_type=jnp.float32,
            )
        for k, row in flat_rows(rows_ref, width):
            held_ref[g, :, 2 * width * k : 2 * width * (k + 1)] = row
        rows_copy(held_ref, out_ref, sems, g).start()

    for g in range(group_total):
        rows_copy(held_ref, out_ref, sems, g).wait()


def widen_kernel(flat_ref, out_ref, held_ref, sems):
    group_total = flat_ref.shape[0]
    for g in range(group_total):
        held_ref[g] = flat_ref[g].astype(jnp.float32)
        rows_copy(held_ref, out_ref, sems, g).start()
    for g in range(group_total):
        rows_copy(held_ref, out_ref, sems, g).wait()


def spread(kernel, name, flat, scratch):
    group_total, pair_total, flat_width = flat.shape
    return pl.pallas_call(
        kernel,
        out_shape=jax.ShapeDtypeStruct((group_total * pair_total, flat_width), jnp.float32),
        in_specs=[pl.BlockSpec(memory_space=pltpu.VMEM)],
        out_specs=pl.BlockSpec(memory_space=pl.ANY),
        scratch_shapes=[
            pltpu.VMEM(flat.shape, jnp.float32),
            pltpu.SemaphoreType.DMA((group_total,)),
            *scratch,
        ],
        compiler_params=pltpu.CompilerParams(vmem_limit_bytes=VMEM_LIMIT),
        cost_estimate=pl.CostEstimate(flops=2**27, bytes_accessed=2**21, transcendentals=0),
        name=name,
    )(flat)


def on_device(basis, stiffness, pair_subs, own_rows, far_rows, pair_count):
    width = basis.shape[1]
    pair_total, tile_count = own_rows.shape
    far_basis = shifted(basis, "sub", 1)
    plan = planned(pair_subs, own_rows, far_rows, pair_count)
    own_part = collect(plan, basis, tile_count)
    flipped = cross_blocks(plan, own_part, far_basis, stiffness, lax.axis_size("grp"))
    gathered = lax.all_to_all(flipped, "grp", 0, 0, axis_index_groups=[ORDER])
    returned = shifted(gathered, "sub", -1)
    block_rows = pltpu.VMEM((pair_total * PITCH, 2 * width), jnp.float32)
    owned_all = spread(turn_kernel, "turned", gathered, [block_rows] * (2 * LANES))
    partner_all = spread(widen_kernel, "widened", returned, [])
    return (owned_all, partner_all)


def solution(mesh):
    return jax.shard_map(
        on_device,
        mesh=mesh,
        in_specs=(
            P(("sub", "grp"), None, None),
            P(("sub", "grp"), None, None, None),
            P(("sub", "grp"), None),
            P(("sub", "grp"), None),
            P(("sub", "grp"), None),
            P(("sub", "grp")),
        ),
        out_specs=(P("sub", None), P("sub", None)),
        check_vma=False,
    )
```

time: 69 us -> 57.7 us (0.84)
  starting transfers between devices: 22.7 us -> 4.85 us
  waiting for transfers between devices: 12.4 us -> 27.7 us
  blocking collectives: 19.2 us -> 15.3 us
  Pallas kernels: 9.7 us -> 6.22 us
  other arithmetic: 1.94 us -> 0.78 us
    ppermute x3 -> x2, starting transfers between devices: 22.7 us -> 4.85 us  [shifted(): return lax.ppermute(block, axis, route)]
    ppermute x3 -> x2, waiting for transfers between devices: 12.4 us -> 27.7 us  [shifted(): return lax.ppermute(block, axis, route)]
    all_to_all x1, blocking collectives: 19.2 us -> 15.3 us  [on_device(): gathered = lax.all_to_all(flipped, 'grp', 0, 0, axis_index_groups=[ORDER])]
    pallas_call x2 -> x1, Pallas kernels: 2.98 us -> 0.81 us  [collect(): pl.pallas_call(collect_kernel, out_shape=jax.ShapeDtypeStruct(shape, basi...]
    pallas_call x1 -> x2, Pallas kernels: 5.2 us -> 3.44 us  [spread(): pl.pallas_call(kernel, out_shape=jax.ShapeDtypeStruct((group_total * pair...]
    convert_element_type x1 -> x0, other arithmetic: 1.04 us -> none  [on_device(): partner_all = returned.reshape(owned_all.shape).astype(jnp.float32)]
    add x3 -> x0, other arithmetic: 0.91 us -> none  [the longest x2 0.83 us: on_device(): wanted = shifted(far_rows + pair_subs[:, 1:2] * tile_total, 'sub', -1)]
    concatenate x0 -> x1, other arithmetic: none -> 0.78 us  [planned(): return jnp.concatenate([pair_subs.T, own_rows.T, far_rows.T, live], axis=0)]
  transfers between devices with their start and end apart: 3 -> 2, of which waited for: 3 -> 2; matrix products, arithmetic and copies ran while one was open for 0% -> 1% of each run, Pallas kernels for 10% -> 6%
where the time goes in v2:
time: 57.7 us; the launch traced here: 57.4 us
  waiting for transfers between devices  27.7 us (48%)
  blocking collectives  15.3 us (27%)
  Pallas kernels  6.22 us (11%)
  starting transfers between devices  4.85 us (8%)
  between operations  1.33 us (2%)
  local copies, waits for them, and re-layouts  1.3 us (2%)
  other arithmetic  0.78 us (1%)
    ppermute x2, waiting for transfers between devices, shifted(): return lax.ppermute(block, axis, route)  27.7 us
    all_to_all x1, blocking collectives, on_device(): gathered = lax.all_to_all(flipped, 'grp', 0, 0, axis_index_groups=[ORDER])  15.3 us
    ppermute x2, starting transfers between devices, shifted(): return lax.ppermute(block, axis, route)  4.85 us
    pallas_call x2, Pallas kernels, spread(): pl.pallas_call(kernel, out_shape=jax.ShapeDtypeStruct((group_total * pair...  3.44 us
    pallas_call x1, Pallas kernels, cross_blocks(): pl.pallas_call(cross_kernel, out_shape=jax.ShapeDtypeStruct((copies, pair...  1.97 us
    unnamed x4, local copies, waits for them, and re-layouts  1.23 us
  transfers between devices with their start and end apart: 2, of which 2 were waited for; matrix products, arithmetic and copies ran while one was open for 1% of the time, Pallas kernels for 6%

profile of v2, /device:TPU:8, one launch (start us, length us, event | category | flops | bytes accessed | tf_op | source)
XLA Modules:
  0.0 57.4 jit_solution(16556221579743240639)
XLA Ops:
  0.6 0.0 copy-start
  0.6 2.1 %collective-permute-start = (bf16[2,64,4096]{2,1,0:T(8,128)(2,1)}, bf16[2,64,4096]{2,1,0:T(8,128)(2,1)S(1)}, u32[]{:S(2)}, u32[]{:S(2)}) collective-permute-start(bf16[2,64,4096]{2,1,0:T(8,128)(2,1)} %basis_ref.1), channel_id=1, source_target_pairs={{760,0},{0,8},{8,16},{16,24},{24,32},{32,40},{40,48},{48,56},{56,6... | collective-permute-start | bytes 3145736 | tf_op jit(solution)/shard_map/ppermute | solution.py:14
  3.3 0.1 pad.3.clone
  3.4 0.8 %add_add_fusion.plan_ref = s32[11,8]{1,0:T(8,128)S(1)} fusion(s32[4,8]{1,0:T(4,128)} %bitcast.4, s32[4,8]{1,0:T(4,128)} %bitcast.5, s32[2,8]{1,0:T(2,128)} %bitcast.6, s32[11]{0:T(128)S(1)} %pad.3.clone), kind=kLoop, calls=%fused_computation | loop fusion | flops 264 | bytes 716 | tf_op jit(solution)/shard_map/concatenate | solution.py:35
  4.2 0.0 copy-start.1
  4.2 1.2 %copy-done.1 = bf16[2,64,4096]{2,1,0:T(8,128)(2,1)S(1)} copy-done((bf16[2,64,4096]{2,1,0:T(8,128)(2,1)S(1)}, bf16[2,64,4096]{2,1,0:T(8,128)(2,1)}, u32[]{:S(2)}) %copy-start.1) | copy-done | bytes 1048600
  5.4 0.8 %collect.1.own_ref = bf16[8,64,512]{2,1,0:T(8,128)(2,1)S(1)} custom-call(s32[11,8]{1,0:T(8,128)S(1)} %add_add_fusion.plan_ref, bf16[2,64,4096]{2,1,0:T(8,128)(2,1)S(1)} %copy-done.1), custom_call_target="tpu_custom_call" | custom-call | flops 134217728 | bytes 4194304 | tf_op jit(solution)/shard_map/collect/pallas_call | solution.py:55
  6.2 23.4 %collective-permute-done.far_ref = bf16[2,64,4096]{2,1,0:T(8,128)(2,1)S(1)} collective-permute-done((bf16[2,64,4096]{2,1,0:T(8,128)(2,1)}, bf16[2,64,4096]{2,1,0:T(8,128)(2,1)S(1)}, u32[]{:S(2)}, u32[]{:S(2)}) %collective-permute-start) | collective-permute-done | bytes 1048608 | tf_op jit(solution)/shard_map/ppermute | solution.py:14
  29.7 0.0 copy-done
  29.7 2.0 %cross_blocks.1 = bf16[8,8,4096]{2,1,0:T(8,128)(2,1)S(1)} custom-call(s32[11,8]{1,0:T(8,128)S(1)} %add_add_fusion.plan_ref, bf16[8,64,512]{2,1,0:T(8,128)(2,1)S(1)} %collect.1.own_ref, bf16[2,64,4096]{2,1,0:T(8,128)(2,1)S(1)} %collective-permute-done.far_ref, bf16[8,4,128,128]{3,2,1,0:T(8,128)(2,1)S(1)} %copy-done), custom_call_target="tpu_custom_call" | custom-call | flops 134217728 | bytes 2097152 | tf_op jit(solution)/shard_map/cross_blocks/pallas_call | solution.py:109
  31.7 15.3 %all_to_all.5.flat_ref = bf16[8,8,4096]{2,1,0:T(8,128)(2,1)S(1)} all-to-all(bf16[8,8,4096]{2,1,0:T(8,128)(2,1)S(1)} %cross_blocks.1), channel_id=1, replica_groups={{5,4,6,3,7,2,0,1},{13,12,14,11,15,10,8,9},{21,20,22,19,23,18,16,17},{29..., dimensions={0} | all-to-all | bytes 1048576 | tf_op jit(solution)/shard_map/all_to_all | solution.py:199
  46.9 2.8 %collective-permute-start.1 = (bf16[8,8,4096]{2,1,0:T(8,128)(2,1)S(1)}, bf16[8,8,4096]{2,1,0:T(8,128)(2,1)S(1)}, u32[]{:S(2)}, u32[]{:S(2)}) collective-permute-start(bf16[8,8,4096]{2,1,0:T(8,128)(2,1)S(1)} %all_to_all.5.flat_ref), channel_id=1, source_target_pairs={{8,0},{16,8},{24,16},{32,24},{40,32},{48,40},{56,48},{64,56},{72,6... | collective-permute-start | bytes 1572872 | tf_op jit(solution)/shard_map/ppermute | solution.py:14
  49.7 2.4 %turned.1 = f32[64,4096]{1,0:T(8,128)} custom-call(bf16[8,8,4096]{2,1,0:T(8,128)(2,1)S(1)} %all_to_all.5.flat_ref), custom_call_target="tpu_custom_call" | custom-call | flops 134217728 | bytes 2097152 | tf_op jit(solution)/shard_map/turned/pallas_call | solution.py:176
  52.1 4.3 %collective-permute-done.1.flat_ref = bf16[8,8,4096]{2,1,0:T(8,128)(2,1)S(1)} collective-permute-done((bf16[8,8,4096]{2,1,0:T(8,128)(2,1)S(1)}, bf16[8,8,4096]{2,1,0:T(8,128)(2,1)S(1)}, u32[]{:S(2)}, u32[]{:S(2)}) %collective-permute-start.1) | collective-permute-done | bytes 524320 | tf_op jit(solution)/shard_map/ppermute | solution.py:14
  56.4 1.0 %widened.1 = f32[64,4096]{1,0:T(8,128)} custom-call(bf16[8,8,4096]{2,1,0:T(8,128)(2,1)S(1)} %collective-permute-done.1.flat_ref), custom_call_target="tpu_custom_call" | custom-call | flops 134217728 | bytes 2097152 | tf_op jit(solution)/shard_map/widened/pallas_call | solution.py:176
Async XLA Ops:
  0.6 29.1 %copy-start = (bf16[8,4,128,128]{3,2,1,0:T(8,128)(2,1)S(1)}, bf16[8,4,128,128]{3,2,1,0:T(8,128)(2,1)}, u32[]{:S(2)}) copy-start(bf16[8,4,128,128]{3,2,1,0:T(8,128)(2,1)} %stiff_ref.1) | copy-start | bytes 3145732
  0.6 29.0 %collective-permute-start = (bf16[2,64,4096]{2,1,0:T(8,128)(2,1)}, bf16[2,64,4096]{2,1,0:T(8,128)(2,1)S(1)}, u32[]{:S(2)}, u32[]{:S(2)}) collective-permute-start(bf16[2,64,4096]{2,1,0:T(8,128)(2,1)} %basis_ref.1), channel_id=1, source_target_pairs={{760,0},{0,8},{8,16},{16,24},{24,32},{32,40},{40,48},{48,56},{56,6... | collective-permute-start | bytes 3145736 | tf_op jit(solution)/shard_map/ppermute | solution.py:14
  4.2 1.2 %copy-start.1 = (bf16[2,64,4096]{2,1,0:T(8,128)(2,1)S(1)}, bf16[2,64,4096]{2,1,0:T(8,128)(2,1)}, u32[]{:S(2)}) copy-start(bf16[2,64,4096]{2,1,0:T(8,128)(2,1)} %basis_ref.1) | copy-start | bytes 3145732
  46.9 9.5 %collective-permute-start.1 = (bf16[8,8,4096]{2,1,0:T(8,128)(2,1)S(1)}, bf16[8,8,4096]{2,1,0:T(8,128)(2,1)S(1)}, u32[]{:S(2)}, u32[]{:S(2)}) collective-permute-start(bf16[8,8,4096]{2,1,0:T(8,128)(2,1)S(1)} %all_to_all.5.flat_ref), channel_id=1, source_target_pairs={{8,0},{16,8},{24,16},{32,24},{40,32},{48,40},{56,48},{64,56},{72,6... | collective-permute-start | bytes 1572872 | tf_op jit(solution)/shard_map/ppermute | solution.py:14

commit v3 on v2

--- a/solution.py
+++ b/solution.py
@@ -18,6 +18,10 @@
 PITCH = 72
 
 
+def block_rows(pair_total, width):
+    return pltpu.VMEM(((pair_total + 1) * PITCH, 2 * width), jnp.float32)
+
+
 def flat_rows(rows_ref, width):
     left = lax.broadcasted_iota(jnp.int32, (8, 2 * width), 1) < width
     for k in range(width // 2):
@@ -27,17 +31,18 @@
 
 
 OWN_SUB, FAR_SUB, OWN_TILES, FAR_TILES, LIVE = 0, 1, 2, 6, 10
+PAIRS = 8
 
 
 def planned(pair_subs, own_rows, far_rows, pair_count):
     pair_total = own_rows.shape[0]
     live = jnp.broadcast_to(pair_count[:, None], (1, pair_total))
-    return jnp.concatenate([pair_subs.T, own_rows.T, far_rows.T, live], axis=0)
+    return jnp.concatenate([pair_subs.T, own_rows.T, far_rows.T, live], axis=0).reshape(-1)
 
 
 def tile(basis_ref, plan_ref, sub_at, tile_at, p):
-    first = pl.multiple_of(plan_ref[tile_at, p] * 128, 128)
-    return basis_ref[plan_ref[sub_at, p], :, pl.ds(first, 128)]
+    first = pl.multiple_of(plan_ref[tile_at * PAIRS + p] * 128, 128)
+    return basis_ref[plan_ref[sub_at * PAIRS + p], :, pl.ds(first, 128)]
 
 
 def collect_kernel(plan_ref, basis_ref, part_ref):
@@ -51,7 +56,7 @@
 
 def collect(plan, basis, tile_count):
     vmem = pl.BlockSpec(memory_space=pltpu.VMEM)
-    shape = (plan.shape[1], basis.shape[1], tile_count * 128)
+    shape = (PAIRS, basis.shape[1], tile_count * 128)
     return pl.pallas_call(
         collect_kernel,
         out_shape=jax.ShapeDtypeStruct(shape, basis.dtype),
@@ -89,7 +94,7 @@
             NT,
             preferred_element_type=jnp.float32,
         )
-        keep = p < plan_ref[LIVE, p]
+        keep = p < plan_ref[LIVE * PAIRS + p]
         rows_ref[p * PITCH : p * PITCH + width, :] = jnp.where(keep, flipped, 0.0)
 
     image = imaged(0)
@@ -111,7 +116,7 @@
         out_shape=jax.ShapeDtypeStruct((copies, pair_total, width * width), jnp.bfloat16),
         in_specs=[pl.BlockSpec(memory_space=pltpu.SMEM), vmem, vmem, vmem],
         out_specs=vmem,
-        scratch_shapes=[pltpu.VMEM((pair_total * PITCH, 2 * width), jnp.float32)],
+        scratch_shapes=[block_rows(pair_total, width)],
         compiler_params=pltpu.CompilerParams(vmem_limit_bytes=VMEM_LIMIT),
         cost_estimate=pl.CostEstimate(flops=2**27, bytes_accessed=2**21, transcendentals=0),
         name="cross_blocks",
@@ -198,8 +203,8 @@
     flipped = cross_blocks(plan, own_part, far_basis, stiffness, lax.axis_size("grp"))
     gathered = lax.all_to_all(flipped, "grp", 0, 0, axis_index_groups=[ORDER])
     returned = shifted(gathered, "sub", -1)
-    block_rows = pltpu.VMEM((pair_total * PITCH, 2 * width), jnp.float32)
-    owned_all = spread(turn_kernel, "turned", gathered, [block_rows] * (2 * LANES))
+    block_scratch = [block_rows(pair_total, width)] * (2 * LANES)
+    owned_all = spread(turn_kernel, "turned", gathered, block_scratch)
     partner_all = spread(widen_kernel, "widened", returned, [])
     return (owned_all, partner_all)
 

time: 57.7 us -> 57.4 us (level)
  local copies, waits for them, and re-layouts: 1.3 us -> 2.1 us
  other arithmetic: 0.78 us -> 0.07 us
    concatenate x1, other arithmetic: 0.78 us -> 0.07 us  [planned(): jnp.concatenate([pair_subs.T, own_rows.T, far_rows.T, live], axis=0)]
    unnamed x4 -> x10, local copies, waits for them, and re-layouts: 1.23 us -> 1.94 us
  transfers between devices with their start and end apart: 2 -> 2, of which waited for: 2 -> 2; matrix products, arithmetic and copies ran while one was open for 1% -> 0% of each run, Pallas kernels for 6% -> 5%
where the time goes in v3:
time: 57.4 us; the launch traced here: 57.2 us
  waiting for transfers between devices  27.7 us (48%)
  blocking collectives  15.3 us (27%)
  Pallas kernels  5.97 us (10%)
  starting transfers between devices  4.72 us (8%)
  local copies, waits for them, and re-layouts  2.1 us (4%)
  between operations  1.32 us (2%)
    ppermute x2, waiting for transfers between devices, shifted(): return lax.ppermute(block, axis, route)  27.7 us
    all_to_all x1, blocking collectives, on_device(): gathered = lax.all_to_all(flipped, 'grp', 0, 0, axis_index_groups=[ORDER])  15.3 us
    ppermute x2, starting transfers between devices, shifted(): return lax.ppermute(block, axis, route)  4.72 us
    pallas_call x2, Pallas kernels, spread(): pl.pallas_call(kernel, out_shape=jax.ShapeDtypeStruct((group_total * pair...  3.45 us
    unnamed x10, local copies, waits for them, and re-layouts  1.94 us
    pallas_call x1, Pallas kernels, cross_blocks(): pl.pallas_call(cross_kernel, out_shape=jax.ShapeDtypeStruct((copies, pair...  1.84 us
  transfers between devices with their start and end apart: 2, of which 2 were waited for; matrix products, arithmetic and copies ran while one was open for 0% of the time, Pallas kernels for 5%

profile of v3, /device:TPU:8, one launch (start us, length us, event | category | flops | bytes accessed | tf_op | source)
XLA Modules:
  0.0 57.2 jit_solution(6448511341338486941)
XLA Ops:
  0.6 1.9 %collective-permute-start = (bf16[2,64,4096]{2,1,0:T(8,128)(2,1)}, bf16[2,64,4096]{2,1,0:T(8,128)(2,1)S(1)}, u32[]{:S(2)}, u32[]{:S(2)}) collective-permute-start(bf16[2,64,4096]{2,1,0:T(8,128)(2,1)} %basis_ref.1), channel_id=1, source_target_pairs={{760,0},{0,8},{8,16},{16,24},{24,32},{32,40},{40,48},{48,56},{56,6... | collective-permute-start | bytes 3145736 | tf_op jit(solution)/shard_map/ppermute | solution.py:14
  3.2 0.1 pad.3.clone
  3.3 0.0 copy-start.3
  3.3 0.0 copy-start.2
  3.3 0.0 copy-start.4
  3.3 0.7 %copy-done.3 = s32[8,4]{0,1:T(4,128)S(1)} copy-done((s32[8,4]{0,1:T(4,128)S(1)}, s32[8,4]{0,1:T(4,128)}, u32[]{:S(2)}) %copy-start.3) | copy-done | bytes 152
  4.0 0.0 copy-done.2
  4.0 0.0 copy-done.4
  4.0 0.1 add_add_fusion
  4.1 0.1 reshape.10.plan_ref
  4.1 0.0 copy-start
  4.2 1.2 %copy-done = bf16[2,64,4096]{2,1,0:T(8,128)(2,1)S(1)} copy-done((bf16[2,64,4096]{2,1,0:T(8,128)(2,1)S(1)}, bf16[2,64,4096]{2,1,0:T(8,128)(2,1)}, u32[]{:S(2)}) %copy-start) | copy-done | bytes 1048600
  5.4 0.0 copy-start.1
  5.4 0.7 %collect.1.own_ref = bf16[8,64,512]{2,1,0:T(8,128)(2,1)S(1)} custom-call(s32[88]{0:T(128)S(1)} %reshape.10.plan_ref, bf16[2,64,4096]{2,1,0:T(8,128)(2,1)S(1)} %copy-done), custom_call_target="tpu_custom_call" | custom-call | flops 134217728 | bytes 4194304 | tf_op jit(solution)/shard_map/collect/pallas_call | solution.py:60
  6.1 23.5 %collective-permute-done.far_ref = bf16[2,64,4096]{2,1,0:T(8,128)(2,1)S(1)} collective-permute-done((bf16[2,64,4096]{2,1,0:T(8,128)(2,1)}, bf16[2,64,4096]{2,1,0:T(8,128)(2,1)S(1)}, u32[]{:S(2)}, u32[]{:S(2)}) %collective-permute-start) | collective-permute-done | bytes 1048608 | tf_op jit(solution)/shard_map/ppermute | solution.py:14
  29.5 0.0 copy-done.1
  29.5 1.8 %cross_blocks.1 = bf16[8,8,4096]{2,1,0:T(8,128)(2,1)S(1)} custom-call(s32[88]{0:T(128)S(1)} %reshape.10.plan_ref, bf16[8,64,512]{2,1,0:T(8,128)(2,1)S(1)} %collect.1.own_ref, bf16[2,64,4096]{2,1,0:T(8,128)(2,1)S(1)} %collective-permute-done.far_ref, bf16[8,4,128,128]{3,2,1,0:T(8,128)(2,1)S(1)} %copy-done.1), custom_call_target="tpu_custom_call" | custom-call | flops 134217728 | bytes 2097152 | tf_op jit(solution)/shard_map/cross_blocks/pallas_call | solution.py:114
  31.4 15.3 %all_to_all.5.flat_ref = bf16[8,8,4096]{2,1,0:T(8,128)(2,1)S(1)} all-to-all(bf16[8,8,4096]{2,1,0:T(8,128)(2,1)S(1)} %cross_blocks.1), channel_id=1, replica_groups={{5,4,6,3,7,2,0,1},{13,12,14,11,15,10,8,9},{21,20,22,19,23,18,16,17},{29..., dimensions={0} | all-to-all | bytes 1048576 | tf_op jit(solution)/shard_map/all_to_all | solution.py:204
  46.7 2.8 %collective-permute-start.1 = (bf16[8,8,4096]{2,1,0:T(8,128)(2,1)S(1)}, bf16[8,8,4096]{2,1,0:T(8,128)(2,1)S(1)}, u32[]{:S(2)}, u32[]{:S(2)}) collective-permute-start(bf16[8,8,4096]{2,1,0:T(8,128)(2,1)S(1)} %all_to_all.5.flat_ref), channel_id=1, source_target_pairs={{8,0},{16,8},{24,16},{32,24},{40,32},{48,40},{56,48},{64,56},{72,6... | collective-permute-start | bytes 1572872 | tf_op jit(solution)/shard_map/ppermute | solution.py:14
  49.5 2.4 %turned.1 = f32[64,4096]{1,0:T(8,128)} custom-call(bf16[8,8,4096]{2,1,0:T(8,128)(2,1)S(1)} %all_to_all.5.flat_ref), custom_call_target="tpu_custom_call" | custom-call | flops 134217728 | bytes 2097152 | tf_op jit(solution)/shard_map/turned/pallas_call | solution.py:181
  51.9 4.3 %collective-permute-done.1.flat_ref = bf16[8,8,4096]{2,1,0:T(8,128)(2,1)S(1)} collective-permute-done((bf16[8,8,4096]{2,1,0:T(8,128)(2,1)S(1)}, bf16[8,8,4096]{2,1,0:T(8,128)(2,1)S(1)}, u32[]{:S(2)}, u32[]{:S(2)}) %collective-permute-start.1) | collective-permute-done | bytes 524320 | tf_op jit(solution)/shard_map/ppermute | solution.py:14
  56.1 1.0 %widened.1 = f32[64,4096]{1,0:T(8,128)} custom-call(bf16[8,8,4096]{2,1,0:T(8,128)(2,1)S(1)} %collective-permute-done.1.flat_ref), custom_call_target="tpu_custom_call" | custom-call | flops 134217728 | bytes 2097152 | tf_op jit(solution)/shard_map/widened/pallas_call | solution.py:181
Async XLA Ops:
  0.6 28.9 %collective-permute-start = (bf16[2,64,4096]{2,1,0:T(8,128)(2,1)}, bf16[2,64,4096]{2,1,0:T(8,128)(2,1)S(1)}, u32[]{:S(2)}, u32[]{:S(2)}) collective-permute-start(bf16[2,64,4096]{2,1,0:T(8,128)(2,1)} %basis_ref.1), channel_id=1, source_target_pairs={{760,0},{0,8},{8,16},{16,24},{24,32},{32,40},{40,48},{48,56},{56,6... | collective-permute-start | bytes 3145736 | tf_op jit(solution)/shard_map/ppermute | solution.py:14
  3.3 0.7 %copy-start.3 = (s32[8,4]{0,1:T(4,128)S(1)}, s32[8,4]{0,1:T(4,128)}, u32[]{:S(2)}) copy-start(s32[8,4]{0,1:T(4,128)} %param.9) | copy-start | bytes 388
  3.3 0.7 %copy-start.2 = (s32[8,4]{0,1:T(4,128)S(1)}, s32[8,4]{0,1:T(4,128)}, u32[]{:S(2)}) copy-start(s32[8,4]{0,1:T(4,128)} %param.10) | copy-start | bytes 388
  3.3 0.7 %copy-start.4 = (s32[8,2]{0,1:T(2,128)S(1)}, s32[8,2]{0,1:T(2,128)}, u32[]{:S(2)}) copy-start(s32[8,2]{0,1:T(2,128)} %param.8) | copy-start | bytes 196
  4.1 1.2 %copy-start = (bf16[2,64,4096]{2,1,0:T(8,128)(2,1)S(1)}, bf16[2,64,4096]{2,1,0:T(8,128)(2,1)}, u32[]{:S(2)}) copy-start(bf16[2,64,4096]{2,1,0:T(8,128)(2,1)} %basis_ref.1) | copy-start | bytes 3145732
  5.4 24.2 %copy-start.1 = (bf16[8,4,128,128]{3,2,1,0:T(8,128)(2,1)S(1)}, bf16[8,4,128,128]{3,2,1,0:T(8,128)(2,1)}, u32[]{:S(2)}) copy-start(bf16[8,4,128,128]{3,2,1,0:T(8,128)(2,1)} %stiff_ref.1) | copy-start | bytes 3145732
  46.7 9.5 %collective-permute-start.1 = (bf16[8,8,4096]{2,1,0:T(8,128)(2,1)S(1)}, bf16[8,8,4096]{2,1,0:T(8,128)(2,1)S(1)}, u32[]{:S(2)}, u32[]{:S(2)}) collective-permute-start(bf16[8,8,4096]{2,1,0:T(8,128)(2,1)S(1)} %all_to_all.5.flat_ref), channel_id=1, source_target_pairs={{8,0},{16,8},{24,16},{32,24},{40,32},{48,40},{56,48},{64,56},{72,6... | collective-permute-start | bytes 1572872 | tf_op jit(solution)/shard_map/ppermute | solution.py:14

commit v4 on v3

--- a/solution.py
+++ b/solution.py
@@ -22,12 +22,11 @@
     return pltpu.VMEM(((pair_total + 1) * PITCH, 2 * width), jnp.float32)
 
 
-def flat_rows(rows_ref, width):
+def flat_row(rows_ref, width, k):
     left = lax.broadcasted_iota(jnp.int32, (8, 2 * width), 1) < width
-    for k in range(width // 2):
-        even = rows_ref[pl.ds(2 * k, 8, stride=PITCH), :]
-        odd = rows_ref[pl.ds(2 * k + 1, 8, stride=PITCH), :]
-        yield k, jnp.where(left, even, odd)
+    even = rows_ref[pl.ds(2 * k, 8, stride=PITCH), :]
+    odd = rows_ref[pl.ds(2 * k + 1, 8, stride=PITCH), :]
+    return jnp.where(left, even, odd)
 
 
 OWN_SUB, FAR_SUB, OWN_TILES, FAR_TILES, LIVE = 0, 1, 2, 6, 10
@@ -102,8 +101,10 @@
         later = imaged(p + 1) if p + 1 < pair_total else None
         crossed(p, image)
         image = later
-    for k, row in flat_rows(rows_ref, width):
-        row = row.astype(out_ref.dtype)
+    half = width // 4
+    for k in range(half):
+        both = [flat_row(rows_ref, width, k), flat_row(rows_ref, width, k + half)]
+        row = jnp.concatenate(both, axis=0).astype(out_ref.dtype)
         for d in range(out_ref.shape[0]):
             out_ref[d, :, 2 * width * k : 2 * width * (k + 1)] = row
 
@@ -113,7 +114,9 @@
     vmem = pl.BlockSpec(memory_space=pltpu.VMEM)
     return pl.pallas_call(
         cross_kernel,
-        out_shape=jax.ShapeDtypeStruct((copies, pair_total, width * width), jnp.bfloat16),
+        out_shape=jax.ShapeDtypeStruct(
+            (copies, 2 * pair_total, width * width // 2), jnp.bfloat16
+        ),
         in_specs=[pl.BlockSpec(memory_space=pltpu.SMEM), vmem, vmem, vmem],
         out_specs=vmem,
         scratch_shapes=[block_rows(pair_total, width)],
@@ -138,18 +141,20 @@
 
 
 def turn_kernel(flat_ref, out_ref, held_ref, sems, *scratch):
-    group_total, pair_total, _ = flat_ref.shape
+    group_total, pair_total, _ = held_ref.shape
     width = scratch[0].shape[1] // 2
+    half = width // 4
     row_at = lax.broadcasted_iota(jnp.int32, (width, 2 * width), 0)
     lane_at = lax.broadcasted_iota(jnp.int32, (width, 2 * width), 1)
     pick = (row_at == lane_at).astype(jnp.bfloat16)
 
     for g in range(group_total):
         split_ref, rows_ref = scratch[2 * (g % LANES) : 2 * (g % LANES) + 2]
-        for k in range(width // 2):
+        for k in range(half):
             both = flat_ref[g, :, 2 * width * k : 2 * width * (k + 1)].astype(jnp.float32)
-            split_ref[pl.ds(2 * k, 8, stride=PITCH), :] = both
-            split_ref[pl.ds(2 * k + 1, 8, stride=PITCH), :] = pltpu.roll(both, width, 1)
+            for at, part in ((k, both[:pair_total]), (k + half, both[pair_total:])):
+                split_ref[pl.ds(2 * at, 8, stride=PITCH), :] = part
+                split_ref[pl.ds(2 * at + 1, 8, stride=PITCH), :] = pltpu.roll(part, width, 1)
         for p in range(pair_total):
             here = slice(p * PITCH, p * PITCH + width)
             matrix = split_ref[here, :].astype(jnp.bfloat16)
@@ -159,7 +164,8 @@
                 NT,
                 preferred_element_type=jnp.float32,
             )
-        for k, row in flat_rows(rows_ref, width):
+        for k in range(width // 2):
+            row = flat_row(rows_ref, width, k)
             held_ref[g, :, 2 * width * k : 2 * width * (k + 1)] = row
         rows_copy(held_ref, out_ref, sems, g).start()
 
@@ -168,23 +174,25 @@
 
 
 def widen_kernel(flat_ref, out_ref, held_ref, sems):
-    group_total = flat_ref.shape[0]
-    for g in range(group_total):
-        held_ref[g] = flat_ref[g].astype(jnp.float32)
+    group_total, pair_total, flat_width = held_ref.shape
+    for g in range(group_total):
+        wide = flat_ref[g].astype(jnp.float32)
+        held_ref[g, :, : flat_width // 2] = wide[:pair_total]
+        held_ref[g, :, flat_width // 2 :] = wide[pair_total:]
         rows_copy(held_ref, out_ref, sems, g).start()
     for g in range(group_total):
         rows_copy(held_ref, out_ref, sems, g).wait()
 
 
 def spread(kernel, name, flat, scratch):
-    group_total, pair_total, flat_width = flat.shape
+    group_total, pair_total, flat_width = flat.shape[0], flat.shape[1] // 2, 2 * flat.shape[2]
     return pl.pallas_call(
         kernel,
         out_shape=jax.ShapeDtypeStruct((group_total * pair_total, flat_width), jnp.float32),
         in_specs=[pl.BlockSpec(memory_space=pltpu.VMEM)],
         out_specs=pl.BlockSpec(memory_space=pl.ANY),
         scratch_shapes=[
-            pltpu.VMEM(flat.shape, jnp.float32),
+            pltpu.VMEM((group_total, pair_total, flat_width), jnp.float32),
             pltpu.SemaphoreType.DMA((group_total,)),
             *scratch,
         ],

time: 57.4 us -> 57.5 us (level)
  no operation moved by 1% of the time
where the time goes in v4:
time: 57.5 us; the launch traced here: 57.2 us
  waiting for transfers between devices  27.7 us (48%)
  blocking collectives  15.3 us (27%)
  Pallas kernels  5.97 us (10%)
  starting transfers between devices  4.73 us (8%)
  local copies, waits for them, and re-layouts  2.1 us (4%)
  between operations  1.32 us (2%)
    ppermute x2, waiting for transfers between devices, shifted(): return lax.ppermute(block, axis, route)  27.7 us
    all_to_all x1, blocking collectives, on_device(): gathered = lax.all_to_all(flipped, 'grp', 0, 0, axis_index_groups=[ORDER])  15.3 us
    ppermute x2, starting transfers between devices, shifted(): return lax.ppermute(block, axis, route)  4.73 us
    pallas_call x2, Pallas kernels, spread(): pl.pallas_call(kernel, out_shape=jax.ShapeDtypeStruct((group_total * pair...  3.45 us
    unnamed x10, local copies, waits for them, and re-layouts  1.94 us
    pallas_call x1, Pallas kernels, cross_blocks(): pl.pallas_call(cross_kernel, out_shape=jax.ShapeDtypeStruct((copies, 2 *...  1.84 us
  transfers between devices with their start and end apart: 2, of which 2 were waited for; matrix products, arithmetic and copies ran while one was open for 0% of the time, Pallas kernels for 5%

profile of v4, /device:TPU:8, one launch (start us, length us, event | category | flops | bytes accessed | tf_op | source)
XLA Modules:
  0.0 57.2 jit_solution(325116917269621186)
XLA Ops:
  0.6 1.9 %collective-permute-start = (bf16[2,64,4096]{2,1,0:T(8,128)(2,1)}, bf16[2,64,4096]{2,1,0:T(8,128)(2,1)S(1)}, u32[]{:S(2)}, u32[]{:S(2)}) collective-permute-start(bf16[2,64,4096]{2,1,0:T(8,128)(2,1)} %basis_ref.1), channel_id=1, source_target_pairs={{760,0},{0,8},{8,16},{16,24},{24,32},{32,40},{40,48},{48,56},{56,6... | collective-permute-start | bytes 3145736 | tf_op jit(solution)/shard_map/ppermute | solution.py:14
  3.2 0.1 pad.3.clone
  3.3 0.0 copy-start.3
  3.3 0.0 copy-start.2
  3.3 0.0 copy-start.4
  3.3 0.7 %copy-done.3 = s32[8,4]{0,1:T(4,128)S(1)} copy-done((s32[8,4]{0,1:T(4,128)S(1)}, s32[8,4]{0,1:T(4,128)}, u32[]{:S(2)}) %copy-start.3) | copy-done | bytes 152
  4.0 0.0 copy-done.2
  4.0 0.0 copy-done.4
  4.0 0.1 add_add_fusion
  4.1 0.1 reshape.10.plan_ref
  4.1 0.0 copy-start
  4.2 1.2 %copy-done = bf16[2,64,4096]{2,1,0:T(8,128)(2,1)S(1)} copy-done((bf16[2,64,4096]{2,1,0:T(8,128)(2,1)S(1)}, bf16[2,64,4096]{2,1,0:T(8,128)(2,1)}, u32[]{:S(2)}) %copy-start) | copy-done | bytes 1048600
  5.4 0.0 copy-start.1
  5.4 0.7 %collect.1.own_ref = bf16[8,64,512]{2,1,0:T(8,128)(2,1)S(1)} custom-call(s32[88]{0:T(128)S(1)} %reshape.10.plan_ref, bf16[2,64,4096]{2,1,0:T(8,128)(2,1)S(1)} %copy-done), custom_call_target="tpu_custom_call" | custom-call | flops 134217728 | bytes 4194304 | tf_op jit(solution)/shard_map/collect/pallas_call | solution.py:59
  6.1 23.5 %collective-permute-done.far_ref = bf16[2,64,4096]{2,1,0:T(8,128)(2,1)S(1)} collective-permute-done((bf16[2,64,4096]{2,1,0:T(8,128)(2,1)}, bf16[2,64,4096]{2,1,0:T(8,128)(2,1)S(1)}, u32[]{:S(2)}, u32[]{:S(2)}) %collective-permute-start) | collective-permute-done | bytes 1048608 | tf_op jit(solution)/shard_map/ppermute | solution.py:14
  29.5 0.0 copy-done.1
  29.5 1.8 %cross_blocks.1 = bf16[8,16,2048]{2,1,0:T(8,128)(2,1)S(1)} custom-call(s32[88]{0:T(128)S(1)} %reshape.10.plan_ref, bf16[8,64,512]{2,1,0:T(8,128)(2,1)S(1)} %collect.1.own_ref, bf16[2,64,4096]{2,1,0:T(8,128)(2,1)S(1)} %collective-permute-done.far_ref, bf16[8,4,128,128]{3,2,1,0:T(8,128)(2,1)S(1)} %copy-done.1), custom_call_target="tpu_custom_call" | custom-call | flops 134217728 | bytes 2097152 | tf_op jit(solution)/shard_map/cross_blocks/pallas_call | solution.py:115
  31.4 15.3 %all_to_all.5.flat_ref = bf16[8,16,2048]{2,1,0:T(8,128)(2,1)S(1)} all-to-all(bf16[8,16,2048]{2,1,0:T(8,128)(2,1)S(1)} %cross_blocks.1), channel_id=1, replica_groups={{5,4,6,3,7,2,0,1},{13,12,14,11,15,10,8,9},{21,20,22,19,23,18,16,17},{29..., dimensions={0} | all-to-all | bytes 1048576 | tf_op jit(solution)/shard_map/all_to_all | solution.py:212
  46.7 2.8 %collective-permute-start.1 = (bf16[8,16,2048]{2,1,0:T(8,128)(2,1)S(1)}, bf16[8,16,2048]{2,1,0:T(8,128)(2,1)S(1)}, u32[]{:S(2)}, u32[]{:S(2)}) collective-permute-start(bf16[8,16,2048]{2,1,0:T(8,128)(2,1)S(1)} %all_to_all.5.flat_ref), channel_id=1, source_target_pairs={{8,0},{16,8},{24,16},{32,24},{40,32},{48,40},{56,48},{64,56},{72,6... | collective-permute-start | bytes 1572872 | tf_op jit(solution)/shard_map/ppermute | solution.py:14
  49.5 2.4 %turned.1 = f32[64,4096]{1,0:T(8,128)} custom-call(bf16[8,16,2048]{2,1,0:T(8,128)(2,1)S(1)} %all_to_all.5.flat_ref), custom_call_target="tpu_custom_call" | custom-call | flops 134217728 | bytes 2097152 | tf_op jit(solution)/shard_map/turned/pallas_call | solution.py:189
  51.9 4.3 %collective-permute-done.1.flat_ref = bf16[8,16,2048]{2,1,0:T(8,128)(2,1)S(1)} collective-permute-done((bf16[8,16,2048]{2,1,0:T(8,128)(2,1)S(1)}, bf16[8,16,2048]{2,1,0:T(8,128)(2,1)S(1)}, u32[]{:S(2)}, u32[]{:S(2)}) %collective-permute-start.1) | collective-permute-done | bytes 524320 | tf_op jit(solution)/shard_map/ppermute | solution.py:14
  56.1 1.0 %widened.1 = f32[64,4096]{1,0:T(8,128)} custom-call(bf16[8,16,2048]{2,1,0:T(8,128)(2,1)S(1)} %collective-permute-done.1.flat_ref), custom_call_target="tpu_custom_call" | custom-call | flops 134217728 | bytes 2097152 | tf_op jit(solution)/shard_map/widened/pallas_call | solution.py:189
Async XLA Ops:
  0.6 28.9 %collective-permute-start = (bf16[2,64,4096]{2,1,0:T(8,128)(2,1)}, bf16[2,64,4096]{2,1,0:T(8,128)(2,1)S(1)}, u32[]{:S(2)}, u32[]{:S(2)}) collective-permute-start(bf16[2,64,4096]{2,1,0:T(8,128)(2,1)} %basis_ref.1), channel_id=1, source_target_pairs={{760,0},{0,8},{8,16},{16,24},{24,32},{32,40},{40,48},{48,56},{56,6... | collective-permute-start | bytes 3145736 | tf_op jit(solution)/shard_map/ppermute | solution.py:14
  3.3 0.7 %copy-start.3 = (s32[8,4]{0,1:T(4,128)S(1)}, s32[8,4]{0,1:T(4,128)}, u32[]{:S(2)}) copy-start(s32[8,4]{0,1:T(4,128)} %param.9) | copy-start | bytes 388
  3.3 0.7 %copy-start.2 = (s32[8,4]{0,1:T(4,128)S(1)}, s32[8,4]{0,1:T(4,128)}, u32[]{:S(2)}) copy-start(s32[8,4]{0,1:T(4,128)} %param.10) | copy-start | bytes 388
  3.3 0.7 %copy-start.4 = (s32[8,2]{0,1:T(2,128)S(1)}, s32[8,2]{0,1:T(2,128)}, u32[]{:S(2)}) copy-start(s32[8,2]{0,1:T(2,128)} %param.8) | copy-start | bytes 196
  4.1 1.2 %copy-start = (bf16[2,64,4096]{2,1,0:T(8,128)(2,1)S(1)}, bf16[2,64,4096]{2,1,0:T(8,128)(2,1)}, u32[]{:S(2)}) copy-start(bf16[2,64,4096]{2,1,0:T(8,128)(2,1)} %basis_ref.1) | copy-start | bytes 3145732
  5.4 24.2 %copy-start.1 = (bf16[8,4,128,128]{3,2,1,0:T(8,128)(2,1)S(1)}, bf16[8,4,128,128]{3,2,1,0:T(8,128)(2,1)}, u32[]{:S(2)}) copy-start(bf16[8,4,128,128]{3,2,1,0:T(8,128)(2,1)} %stiff_ref.1) | copy-start | bytes 3145732
  46.7 9.5 %collective-permute-start.1 = (bf16[8,16,2048]{2,1,0:T(8,128)(2,1)S(1)}, bf16[8,16,2048]{2,1,0:T(8,128)(2,1)S(1)}, u32[]{:S(2)}, u32[]{:S(2)}) collective-permute-start(bf16[8,16,2048]{2,1,0:T(8,128)(2,1)S(1)} %all_to_all.5.flat_ref), channel_id=1, source_target_pairs={{8,0},{16,8},{24,16},{32,24},{40,32},{48,40},{56,48},{64,56},{72,6... | collective-permute-start | bytes 1572872 | tf_op jit(solution)/shard_map/ppermute | solution.py:14

commit v5 on v4

--- a/solution.py
+++ b/solution.py
@@ -86,13 +86,8 @@
         )
 
     def crossed(p, image):
-        own = own_ref[p]
-        flipped = lax.dot_general(
-            image,
-            jnp.concatenate([own, own], axis=0),
-            NT,
-            preferred_element_type=jnp.float32,
-        )
+        flipped = lax.dot_general(image, own_ref[p], NT, preferred_element_type=jnp.float32)
+        flipped = jnp.concatenate([flipped, flipped], axis=1)
         keep = p < plan_ref[LIVE * PAIRS + p]
         rows_ref[p * PITCH : p * PITCH + width, :] = jnp.where(keep, flipped, 0.0)
 

time: 57.5 us -> 57.3 us (level)
  no operation moved by 1% of the time
where the time goes in v5:
time: 57.3 us; the launch traced here: 57.1 us
  waiting for transfers between devices  27.7 us (48%)
  blocking collectives  15.3 us (27%)
  Pallas kernels  5.85 us (10%)
  starting transfers between devices  4.73 us (8%)
  local copies, waits for them, and re-layouts  2.1 us (4%)
  between operations  1.32 us (2%)
    ppermute x2, waiting for transfers between devices, shifted(): return lax.ppermute(block, axis, route)  27.7 us
    all_to_all x1, blocking collectives, on_device(): gathered = lax.all_to_all(flipped, 'grp', 0, 0, axis_index_groups=[ORDER])  15.3 us
    ppermute x2, starting transfers between devices, shifted(): return lax.ppermute(block, axis, route)  4.73 us
    pallas_call x2, Pallas kernels, spread(): pl.pallas_call(kernel, out_shape=jax.ShapeDtypeStruct((group_total * pair...  3.45 us
    unnamed x10, local copies, waits for them, and re-layouts  1.94 us
    pallas_call x1, Pallas kernels, cross_blocks(): pl.pallas_call(cross_kernel, out_shape=jax.ShapeDtypeStruct((copies, 2 *...  1.72 us
  transfers between devices with their start and end apart: 2, of which 2 were waited for; matrix products, arithmetic and copies ran while one was open for 0% of the time, Pallas kernels for 5%

profile of v5, /device:TPU:8, one launch (start us, length us, event | category | flops | bytes accessed | tf_op | source)
XLA Modules:
  0.0 57.1 jit_solution(6748804267731228682)
XLA Ops:
  0.6 1.9 %collective-permute-start = (bf16[2,64,4096]{2,1,0:T(8,128)(2,1)}, bf16[2,64,4096]{2,1,0:T(8,128)(2,1)S(1)}, u32[]{:S(2)}, u32[]{:S(2)}) collective-permute-start(bf16[2,64,4096]{2,1,0:T(8,128)(2,1)} %basis_ref.1), channel_id=1, source_target_pairs={{760,0},{0,8},{8,16},{16,24},{24,32},{32,40},{40,48},{48,56},{56,6... | collective-permute-start | bytes 3145736 | tf_op jit(solution)/shard_map/ppermute | solution.py:14
  3.2 0.1 pad.3.clone
  3.3 0.0 copy-start.3
  3.3 0.0 copy-start.2
  3.3 0.0 copy-start.4
  3.3 0.7 %copy-done.3 = s32[8,4]{0,1:T(4,128)S(1)} copy-done((s32[8,4]{0,1:T(4,128)S(1)}, s32[8,4]{0,1:T(4,128)}, u32[]{:S(2)}) %copy-start.3) | copy-done | bytes 152
  4.0 0.0 copy-done.2
  4.0 0.0 copy-done.4
  4.0 0.1 add_add_fusion
  4.1 0.1 reshape.10.plan_ref
  4.1 0.0 copy-start
  4.2 1.2 %copy-done = bf16[2,64,4096]{2,1,0:T(8,128)(2,1)S(1)} copy-done((bf16[2,64,4096]{2,1,0:T(8,128)(2,1)S(1)}, bf16[2,64,4096]{2,1,0:T(8,128)(2,1)}, u32[]{:S(2)}) %copy-start) | copy-done | bytes 1048600
  5.4 0.0 copy-start.1
  5.4 0.7 %collect.1.own_ref = bf16[8,64,512]{2,1,0:T(8,128)(2,1)S(1)} custom-call(s32[88]{0:T(128)S(1)} %reshape.10.plan_ref, bf16[2,64,4096]{2,1,0:T(8,128)(2,1)S(1)} %copy-done), custom_call_target="tpu_custom_call" | custom-call | flops 134217728 | bytes 4194304 | tf_op jit(solution)/shard_map/collect/pallas_call | solution.py:59
  6.1 23.5 %collective-permute-done.far_ref = bf16[2,64,4096]{2,1,0:T(8,128)(2,1)S(1)} collective-permute-done((bf16[2,64,4096]{2,1,0:T(8,128)(2,1)}, bf16[2,64,4096]{2,1,0:T(8,128)(2,1)S(1)}, u32[]{:S(2)}, u32[]{:S(2)}) %collective-permute-start) | collective-permute-done | bytes 1048608 | tf_op jit(solution)/shard_map/ppermute | solution.py:14
  29.5 0.0 copy-done.1
  29.5 1.7 %cross_blocks.1 = bf16[8,16,2048]{2,1,0:T(8,128)(2,1)S(1)} custom-call(s32[88]{0:T(128)S(1)} %reshape.10.plan_ref, bf16[8,64,512]{2,1,0:T(8,128)(2,1)S(1)} %collect.1.own_ref, bf16[2,64,4096]{2,1,0:T(8,128)(2,1)S(1)} %collective-permute-done.far_ref, bf16[8,4,128,128]{3,2,1,0:T(8,128)(2,1)S(1)} %copy-done.1), custom_call_target="tpu_custom_call" | custom-call | flops 134217728 | bytes 2097152 | tf_op jit(solution)/shard_map/cross_blocks/pallas_call | solution.py:110
  31.3 15.3 %all_to_all.5.flat_ref = bf16[8,16,2048]{2,1,0:T(8,128)(2,1)S(1)} all-to-all(bf16[8,16,2048]{2,1,0:T(8,128)(2,1)S(1)} %cross_blocks.1), channel_id=1, replica_groups={{5,4,6,3,7,2,0,1},{13,12,14,11,15,10,8,9},{21,20,22,19,23,18,16,17},{29..., dimensions={0} | all-to-all | bytes 1048576 | tf_op jit(solution)/shard_map/all_to_all | solution.py:207
  46.5 2.8 %collective-permute-start.1 = (bf16[8,16,2048]{2,1,0:T(8,128)(2,1)S(1)}, bf16[8,16,2048]{2,1,0:T(8,128)(2,1)S(1)}, u32[]{:S(2)}, u32[]{:S(2)}) collective-permute-start(bf16[8,16,2048]{2,1,0:T(8,128)(2,1)S(1)} %all_to_all.5.flat_ref), channel_id=1, source_target_pairs={{8,0},{16,8},{24,16},{32,24},{40,32},{48,40},{56,48},{64,56},{72,6... | collective-permute-start | bytes 1572872 | tf_op jit(solution)/shard_map/ppermute | solution.py:14
  49.4 2.4 %turned.1 = f32[64,4096]{1,0:T(8,128)} custom-call(bf16[8,16,2048]{2,1,0:T(8,128)(2,1)S(1)} %all_to_all.5.flat_ref), custom_call_target="tpu_custom_call" | custom-call | flops 134217728 | bytes 2097152 | tf_op jit(solution)/shard_map/turned/pallas_call | solution.py:184
  51.8 4.3 %collective-permute-done.1.flat_ref = bf16[8,16,2048]{2,1,0:T(8,128)(2,1)S(1)} collective-permute-done((bf16[8,16,2048]{2,1,0:T(8,128)(2,1)S(1)}, bf16[8,16,2048]{2,1,0:T(8,128)(2,1)S(1)}, u32[]{:S(2)}, u32[]{:S(2)}) %collective-permute-start.1) | collective-permute-done | bytes 524320 | tf_op jit(solution)/shard_map/ppermute | solution.py:14
  56.0 1.0 %widened.1 = f32[64,4096]{1,0:T(8,128)} custom-call(bf16[8,16,2048]{2,1,0:T(8,128)(2,1)S(1)} %collective-permute-done.1.flat_ref), custom_call_target="tpu_custom_call" | custom-call | flops 134217728 | bytes 2097152 | tf_op jit(solution)/shard_map/widened/pallas_call | solution.py:184
Async XLA Ops:
  0.6 28.9 %collective-permute-start = (bf16[2,64,4096]{2,1,0:T(8,128)(2,1)}, bf16[2,64,4096]{2,1,0:T(8,128)(2,1)S(1)}, u32[]{:S(2)}, u32[]{:S(2)}) collective-permute-start(bf16[2,64,4096]{2,1,0:T(8,128)(2,1)} %basis_ref.1), channel_id=1, source_target_pairs={{760,0},{0,8},{8,16},{16,24},{24,32},{32,40},{40,48},{48,56},{56,6... | collective-permute-start | bytes 3145736 | tf_op jit(solution)/shard_map/ppermute | solution.py:14
  3.3 0.7 %copy-start.3 = (s32[8,4]{0,1:T(4,128)S(1)}, s32[8,4]{0,1:T(4,128)}, u32[]{:S(2)}) copy-start(s32[8,4]{0,1:T(4,128)} %param.9) | copy-start | bytes 388
  3.3 0.7 %copy-start.2 = (s32[8,4]{0,1:T(4,128)S(1)}, s32[8,4]{0,1:T(4,128)}, u32[]{:S(2)}) copy-start(s32[8,4]{0,1:T(4,128)} %param.10) | copy-start | bytes 388
  3.3 0.7 %copy-start.4 = (s32[8,2]{0,1:T(2,128)S(1)}, s32[8,2]{0,1:T(2,128)}, u32[]{:S(2)}) copy-start(s32[8,2]{0,1:T(2,128)} %param.8) | copy-start | bytes 196
  4.1 1.2 %copy-start = (bf16[2,64,4096]{2,1,0:T(8,128)(2,1)S(1)}, bf16[2,64,4096]{2,1,0:T(8,128)(2,1)}, u32[]{:S(2)}) copy-start(bf16[2,64,4096]{2,1,0:T(8,128)(2,1)} %basis_ref.1) | copy-start | bytes 3145732
  5.4 24.2 %copy-start.1 = (bf16[8,4,128,128]{3,2,1,0:T(8,128)(2,1)S(1)}, bf16[8,4,128,128]{3,2,1,0:T(8,128)(2,1)}, u32[]{:S(2)}) copy-start(bf16[8,4,128,128]{3,2,1,0:T(8,128)(2,1)} %stiff_ref.1) | copy-start | bytes 3145732
  46.5 9.5 %collective-permute-start.1 = (bf16[8,16,2048]{2,1,0:T(8,128)(2,1)S(1)}, bf16[8,16,2048]{2,1,0:T(8,128)(2,1)S(1)}, u32[]{:S(2)}, u32[]{:S(2)}) collective-permute-start(bf16[8,16,2048]{2,1,0:T(8,128)(2,1)S(1)} %all_to_all.5.flat_ref), channel_id=1, source_target_pairs={{8,0},{16,8},{24,16},{32,24},{40,32},{48,40},{56,48},{64,56},{72,6... | collective-permute-start | bytes 1572872 | tf_op jit(solution)/shard_map/ppermute | solution.py:14
